TPU v7x, 1024 devices: a whole 8x8x8 slice. The times are simulated.
1024 devices in a mesh: section: 16 (over z, y_lo), dp: 8 (over x), tensor: 8 (over y_hi, core).
Axes of the slice: x: 8, y: 8 (y_hi: 4, y_lo: 2; y = y_hi * 2 + y_lo), z: 8, core: 2. Of those that a mesh axis runs over, the one named last changes fastest.
Arguments:
- hidden: bfloat16 [16, 8, 256, 16384], P('section', 'dp', None, 'tensor'), may hold values from -80 to 80
- owner: int32 [16, 8, 256, 1], P('section', 'dp'), may hold values from 0 to 7; in each aligned block of 256 rows (0 to 255, 256 to 511, ..., all dimensions but the last counted through in order) at most 48 rows name the same one
- start: int32 [16, 8], P('section', 'dp'), may hold values from 0 to 1792
- live: int32 [16, 8], P('section', 'dp'), may hold values from 128 to 256
- norm_gain: float32 [16, 16384], P('section', 'tensor'), may hold values from 0.5 to 1.5
- w_kv: bfloat16 [16, 16384, 2048], P('section', 'tensor'), may hold values from -0.046875 to 0.046875
Outputs:
- kv_cache: bfloat16 [16, 8, 384, 2048], P('section', 'dp', None, 'tensor')
Inputs may be any that keep to these rules, and one draw needn't show every extreme that they name: `owner`: among the 256 rows of one block no group is named by more than 48 rows, and some block names one group exactly 48 times. The live rows of a block are its first ones.
All inputs are finite; a program needn't handle non-finite values.
Results may differ from a plain program's by a relative error of at most 0.0049.
Values may be sent and summed in bfloat16 or wider, within the bound.
A program may use at most 64 MiB of HBM per device.

v0:
```python
import jax
import jax.numpy as jnp
from jax import lax
from jax.sharding import PartitionSpec as P

D = 16384
HD = 128


EPSILON = 1e-05
ROPE_BASE = 500000.0


def shifted(block, axis, distance):
    devices = range(lax.axis_size(axis))
    route = [(i - distance, i) for i in devices if i - distance in devices]
    return lax.ppermute(block, axis, route)


def rotate_keys(kv_rows, positions):
    half_size = kv_rows.shape[3] // 2
    head_size = kv_rows.shape[3]
    inverse = ROPE_BASE ** (-(jnp.arange(half_size, dtype=jnp.float32) * 2.0 / head_size))
    angles = positions.astype(jnp.float32)[:, None] * inverse[None, :]
    cosines = jnp.cos(angles)[:, None, :]
    sines = jnp.sin(angles)[:, None, :]
    key_part = kv_rows[:, :, 0, :]
    front_half = key_part[..., :half_size]
    back_half = key_part[..., half_size:]
    rotated = jnp.concatenate(
        [front_half * cosines - back_half * sines, back_half * cosines + front_half * sines],
        axis=-1,
    )
    return jnp.stack([rotated, kv_rows[:, :, 1, :]], axis=2)


def per_device(hidden, owner, start, live, norm_gain, w_kv):
    groups = lax.axis_size("dp")
    tensor = lax.axis_size("tensor")
    tok_count = hidden.shape[2]
    local_width = hidden.shape[3]
    capacity = 3 * tok_count // (2 * groups)
    slot_count = capacity * groups
    tok_rows = hidden[0, 0]
    target = owner[0, 0, :, 0]
    row_index = jnp.arange(tok_count, dtype=jnp.int32)
    row_alive = row_index < live[0, 0]
    onehot = (
        (target[:, None] == jnp.arange(groups, dtype=jnp.int32)[None, :]) & row_alive[:, None]
    ).astype(jnp.int32)
    row_rank = jnp.sum((jnp.cumsum(onehot, axis=0) - onehot) * onehot, axis=1)
    row_slot = jnp.where(row_alive, target * capacity + row_rank, slot_count)
    placing = row_slot[None, :] == jnp.arange(slot_count, dtype=jnp.int32)[:, None]
    packed = jnp.dot(
        placing.astype(jnp.bfloat16), tok_rows, preferred_element_type=jnp.float32
    ).astype(jnp.bfloat16)
    packed = packed.reshape(groups, capacity, local_width)
    position = start[0, 0] + row_index
    packed_pos = jnp.sum(jnp.where(placing, position[None, :], 0), axis=1).reshape(groups, capacity)
    routed = (
        lax.all_to_all(packed, "dp", split_axis=0, concat_axis=0, tiled=True),
        lax.all_to_all(packed_pos, "dp", split_axis=0, concat_axis=0, tiled=True),
    )
    arrived, arrived_pos = shifted((routed[0], routed[1]), "section", 1)
    arrived = arrived.reshape(slot_count, local_width)
    arrived_pos = arrived_pos.reshape(slot_count)
    widened = arrived.astype(jnp.float32)
    sum_sq = lax.psum(jnp.sum(widened * widened, axis=1), "tensor")
    normed = (widened * norm_gain[0] * lax.rsqrt(sum_sq / D + EPSILON)[:, None]).astype(
        jnp.bfloat16
    )
    weight = w_kv[0]
    kv_width = weight.shape[1]
    local_cols = kv_width // tensor
    summed = lax.psum_scatter(
        lax.dot_general(
            weight, normed, (((0,), (1,)), ((), ())), preferred_element_type=jnp.float32
        ),
        "tensor",
        scatter_dimension=0,
        tiled=True,
    )
    local_kv = summed.T.reshape(slot_count, local_cols // (2 * HD), 2, HD)
    result = rotate_keys(local_kv, arrived_pos).reshape(slot_count, local_cols).astype(jnp.bfloat16)
    return result.reshape(1, 1, slot_count, local_cols)


def solution(mesh):
    in_specs = (
        P("section", "dp", None, "tensor"),
        P("section", "dp", None, None),
        P("section", "dp"),
        P("section", "dp"),
        P("section", "tensor"),
        P("section", "tensor", None),
    )
    out_specs = P("section", "dp", None, "tensor")
    return jax.shard_map(
        per_device, mesh=mesh, in_specs=in_specs, out_specs=out_specs, check_vma=False
    )
```

profile of v0, /device:TPU:8, one launch (start us, length us, event | category | flops | bytes accessed | tf_op | source)
XLA Modules:
  0.0 192.7 jit_solution(13037670386899562614)
XLA Ops:
  6.5 0.0 copy-start
  6.5 0.0 reduce-scatter.2.cloned.1.call-start
  7.3 0.7 fusion.22
  8.0 0.6 reduce-window.6
  8.6 0.2 slice_reduce_fusion
  9.5 0.8 fusion.19
  10.2 0.7 iota_add_fusion
  10.9 0.0 copy-done
  10.9 0.0 copy-start.1
  10.9 0.6 convolution_convert_fusion
  11.5 41.6 %all_to_all.17 = bf16[8,48,2048]{2,1,0:T(8,128)(2,1)S(1)} all-to-all(bf16[8,48,2048]{2,1,0:T(8,128)(2,1)S(1)} %bitcast.38), channel_id=1, replica_groups=mesh['section'=16,'dp'=8,'tensor'=8] {'dp'}, dimensions={0} | all-to-all | bytes 3145728 | tf_op jit(solution)/shard_map/all_to_all | solution.py:61
  53.1 3.7 %collective-permute-start = (bf16[8,48,2048]{2,1,0:T(8,128)(2,1)S(1)}, bf16[8,48,2048]{2,1,0:T(8,128)(2,1)S(1)}, u32[]{:S(2)}, u32[]{:S(2)}) collective-permute-start(bf16[8,48,2048]{2,1,0:T(8,128)(2,1)S(1)} %all_to_all.17), channel_id=1, source_target_pairs={{0,64},{64,128},{128,192},{192,256},{256,320},{320,384},{384,448},... | collective-permute-start | bytes 4718600 | tf_op jit(solution)/shard_map/ppermute | solution.py:17
  56.8 32.8 %collective-permute-done = bf16[8,48,2048]{2,1,0:T(8,128)(2,1)S(1)} collective-permute-done((bf16[8,48,2048]{2,1,0:T(8,128)(2,1)S(1)}, bf16[8,48,2048]{2,1,0:T(8,128)(2,1)S(1)}, u32[]{:S(2)}, u32[]{:S(2)}) %collective-permute-start) | collective-permute-done | bytes 1572896 | tf_op jit(solution)/shard_map/ppermute | solution.py:17
  89.6 0.4 fusion.4
  90.0 0.1 reduce_sum.31
  90.1 16.0 %psum.7 = f32[384]{0:T(512)S(1)} all-reduce(f32[384]{0:T(512)S(1)} %reduce_sum.31), channel_id=1, replica_groups=mesh['section'=16,'dp'=8,'tensor'=8] {'tensor'}, use_global_device_ids=true, to_apply=%region_4.5 | all-reduce | flops 384 | bytes 3072 | tf_op jit(solution)/shard_map/psum | solution.py:68
  106.1 0.1 mul.85
  106.2 0.0 copy-done.1
  106.2 0.4 fusion.3
  106.6 8.5 %fusion.5 = f32[2048,384]{0,1:T(8,128)} fusion(bf16[384,2048]{1,0:T(8,128)(2,1)S(1)} %bitcast.39, bf16[1,2048,2048]{2,1,0:T(8,128)(2,1)} %param.11), kind=kOutput, calls=%fused_computation.7 | convolution fusion | flops 3221225472 | bytes 13107200 | tf_op jit(solution)/shard_map/dot_general | solution.py:76
  115.1 0.0 reduce-scatter.2.cloned.1.call-update
  115.1 0.1 select_reduce_fusion
  115.3 0.1 all_to_all.12
  115.4 9.6 %all_to_all.18 = s32[8,1,48]{2,1,0:T(1,128)S(1)} all-to-all(s32[8,1,48]{2,1,0:T(1,128)S(1)} %all_to_all.12), channel_id=1, replica_groups=mesh['section'=16,'dp'=8,'tensor'=8] {'dp'}, dimensions={0} | all-to-all | bytes 3072 | tf_op jit(solution)/shard_map/all_to_all | solution.py:62
  125.0 5.9 %collective-permute-start.1 = (s32[8,48]{1,0:T(8,128)S(1)}, s32[8,48]{1,0:T(8,128)S(1)}, u32[]{:S(2)}, u32[]{:S(2)}) collective-permute-start(s32[8,48]{1,0:T(8,128)S(1)} %bitcast.48), channel_id=1, source_target_pairs={{0,64},{64,128},{128,192},{192,256},{256,320},{320,384},{384,448},... | collective-permute-start | bytes 4616 | tf_op jit(solution)/shard_map/ppermute | solution.py:17
  130.9 1.3 collective-permute-done.1
  132.2 0.1 convert_element_type.50
  132.2 51.1 %reduce-scatter.2.cloned.1.call-done = f32[256,384]{0,1:T(8,128)} async-done(((f32[2048,384]{0,1:T(8,128)}), f32[256,384]{0,1:T(8,128)}) %reduce-scatter.2.cloned.1.call-update) | async-done | bytes 393232 | tf_op jit(solution)/shard_map/reduce_scatter | solution.py:75
  183.4 1.2 copy.18
  184.6 0.4 fusion.15
  185.1 0.8 copy.21
  (11 shorter events, 0.1 us)
Async XLA Ops:
  6.5 4.4 %copy-start = (bf16[1,1,256,2048]{3,2,1,0:T(8,128)(2,1)S(1)}, bf16[1,1,256,2048]{3,2,1,0:T(8,128)(2,1)}, u32[]{:S(2)}) copy-start(bf16[1,1,256,2048]{3,2,1,0:T(8,128)(2,1)} %param.6) | copy-start | bytes 3145732
  6.5 176.8 %reduce-scatter.2.cloned.1.call-start = ((), (), s32[]{:S(2)}) async-start(), calls=%async_computation.3 | async-start | bytes 3538944 | tf_op jit(solution)/shard_map/reduce_scatter | solution.py:75
  10.9 95.3 %copy-start.1 = (f32[1,2048]{1,0:T(1,128)S(1)}, f32[1,2048]{1,0:T(1,128)}, u32[]{:S(2)}) copy-start(f32[1,2048]{1,0:T(1,128)} %param.10) | copy-start | bytes 24580
  53.1 36.5 %collective-permute-start = (bf16[8,48,2048]{2,1,0:T(8,128)(2,1)S(1)}, bf16[8,48,2048]{2,1,0:T(8,128)(2,1)S(1)}, u32[]{:S(2)}, u32[]{:S(2)}) collective-permute-start(bf16[8,48,2048]{2,1,0:T(8,128)(2,1)S(1)} %all_to_all.17), channel_id=1, source_target_pairs={{0,64},{64,128},{128,192},{192,256},{256,320},{320,384},{384,448},... | collective-permute-start | bytes 4718600 | tf_op jit(solution)/shard_map/ppermute | solution.py:17
  125.0 7.2 %collective-permute-start.1 = (s32[8,48]{1,0:T(8,128)S(1)}, s32[8,48]{1,0:T(8,128)S(1)}, u32[]{:S(2)}, u32[]{:S(2)}) collective-permute-start(s32[8,48]{1,0:T(8,128)S(1)} %bitcast.48), channel_id=1, source_target_pairs={{0,64},{64,128},{128,192},{192,256},{256,320},{320,384},{384,448},... | collective-permute-start | bytes 4616 | tf_op jit(solution)/shard_map/ppermute | solution.py:17
Sparse Core Ops, SparseCore 0:
  115.3 68.0 reduce-scatter.1
where the time goes:
time: 193 us
  waiting for transfers between devices  85.2 us (44%)
  blocking collectives  67.2 us (35%)
  between operations  14.9 us (8%)
  starting transfers between devices  9.53 us (5%)
  matrix products  9.06 us (5%)
  other arithmetic  4.22 us (2%)
  local copies, waits for them, and re-layouts  2.56 us (1%)
    reduce_scatter x1, waiting for transfers between devices, per_device(): lax.psum_scatter(lax.dot_general(weight, normed, (((0,), (1,)), ((), ()))...  51.1 us
    all_to_all x1, blocking collectives, per_device(): lax.all_to_all(packed, 'dp', split_axis=0, concat_axis=0, tiled=True)  41.6 us
    ppermute x2, waiting for transfers between devices, shifted(): return lax.ppermute(block, axis, route)  34.1 us
    psum x1, blocking collectives, per_device(): sum_sq = lax.psum(jnp.sum(widened * widened, axis=1), 'tensor')  16 us
    all_to_all x1, blocking collectives, per_device(): lax.all_to_all(packed_pos, 'dp', split_axis=0, concat_axis=0, tiled=True)  9.6 us
    ppermute x2, starting transfers between devices, shifted(): return lax.ppermute(block, axis, route)  9.53 us
    dot_general x1, matrix products, per_device(): lax.dot_general(weight, normed, (((0,), (1,)), ((), ())), preferred_eleme...  8.48 us
  transfers between devices with their start and end apart: 3, of which 3 were waited for; matrix products, arithmetic and copies ran while one was open for 0% of the time, Pallas kernels for 0%

commit v1 on v0

v1 whole, which is shorter than its diff:
```python
import functools
import math

import jax
import jax.numpy as jnp
import numpy as np
from jax import lax
from jax.experimental import pallas as pl
from jax.experimental.pallas import tpu as pltpu
from jax.sharding import PartitionSpec as P

HD = 128
EPSILON = 1e-05
ROPE_BASE = 500000.0
F32 = jnp.float32
BF16 = jnp.bfloat16
I32 = jnp.int32


def feature_chunks(width):
    quarter = width // 4
    if quarter % 256:
        return [(0, width // 2), (width // 2, width // 2)]
    cuts = [quarter, quarter, quarter, quarter // 2, quarter // 2]
    return [(sum(cuts[:i]), cut) for i, cut in enumerate(cuts)]


def dot(a, b):
    return jnp.dot(a, b, preferred_element_type=F32)


def kernel(
    sizes,
    hidden,
    owner,
    start,
    live,
    gain,
    inverse,
    weight,
    out,
    own_rows,
    rows,
    w_vmem,
    total,
    ssq_out,
    ssq_in,
    meta_out,
    meta_in,
    scale_ref,
    cos_ref,
    sin_ref,
    place_ref,
    pair_out,
    pair_in,
    hop_out,
    hop_in,
    late_ref,
    packed,
    local_sem,
    shift_sem,
    ssq_sem,
    meta_sem,
    pair_sem,
    hop_sem,
    route_sem,
    keep_sem,
):
    n_section, n_dp, n_tensor, d_model = sizes
    n_ring = n_tensor // 2
    tok, width = own_rows.shape
    slots = place_ref.shape[0]
    cap = slots // n_dp
    half = tok // 2
    chunks = feature_chunks(width)
    sec, dp, ten = lax.axis_index("section"), lax.axis_index("dp"), lax.axis_index("tensor")
    ring, core = ten // 2, ten % 2
    after = (sec + 1) % n_section
    before = (sec + n_section - 1) % n_section
    sibling = (sec, dp, ring * 2 + 1 - core)
    right = (sec, dp, ((ring + 1) % n_ring) * 2 + core)
    left = (sec, dp, ((ring + n_ring - 1) % n_ring) * 2 + core)

    def remote(src, dst, sems, index, device, arrive=None):
        index = index if isinstance(index, tuple) else (index,)
        arrive = index if arrive is None else arrive
        return pltpu.make_async_remote_copy(
            src_ref=src,
            dst_ref=dst,
            send_sem=sems.at[(0, *index)],
            recv_sem=sems.at[(1, *arrive)],
            device_id=device,
            device_id_type=pl.DeviceIdType.MESH,
        )

    barrier = pltpu.get_barrier_semaphore()
    greeted = [(before, dp, t) for t in range(n_tensor)] + [sibling, right, left]
    greeted += [(sec, (dp + k) % n_dp, ten) for k in range(1, n_dp)]
    for device in greeted:
        pl.semaphore_signal(barrier, inc=1, device_id=device, device_id_type=pl.DeviceIdType.MESH)

    take_rows = pltpu.make_async_copy(hidden.at[0, 0], own_rows, local_sem.at[0])
    take_rows.start()
    take_w = []
    for j, (at, wide) in enumerate(chunks):
        part = pl.ds(at, wide)
        take_w.append(
            pltpu.make_async_copy(weight.at[0, part], w_vmem.at[part], local_sem.at[1 + j])
        )
        take_w[-1].start()

    row_id = lax.broadcasted_iota(I32, (8, tok), 0)
    meta_out[...] = jnp.where(row_id == 0, owner[...], jnp.where(row_id == 1, start[0, 0], live[0, 0]))
    pl.semaphore_wait(barrier, len(greeted))

    shifts = []
    for j, (at, wide) in enumerate(chunks):
        part = pl.ds(at, wide)
        shifts.append(
            remote(hidden.at[0, 0, :, part], rows.at[:, part], shift_sem, j, (after, dp, ten))
        )
        shifts[-1].start()
    send_meta = remote(meta_out, meta_in, meta_sem, 0, (after, dp, ten))
    send_meta.start()

    take_rows.wait()
    squares = jnp.zeros((tok, HD), F32)
    for k in range(width // HD):
        piece = own_rows[:, k * HD : (k + 1) * HD].astype(F32)
        squares = squares + piece * piece
    ssq_out[...] = jnp.sum(squares.T, axis=0, keepdims=True)
    send_ssq = []
    for k in range(n_tensor):
        send_ssq.append(remote(ssq_out, ssq_in.at[ten], ssq_sem, k, (after, dp, k), (ten,)))
        send_ssq[-1].start()

    send_meta.wait_recv()
    own_row = meta_in[0:1, :]
    alive = lax.broadcasted_iota(I32, (1, tok), 1) < jnp.where(sec > 0, meta_in[2:3, :], 0)
    named = (lax.broadcasted_iota(I32, (16, tok), 0) == own_row) & alive
    named = jnp.where(named, 1.0, 0.0)
    earlier = lax.broadcasted_iota(I32, (tok, tok), 0) < lax.broadcasted_iota(I32, (tok, tok), 1)
    ranks = dot(named.astype(BF16), jnp.where(earlier, 1.0, 0.0).astype(BF16))
    rank = jnp.sum(ranks * named, axis=0, keepdims=True).astype(I32)
    slot = jnp.where(alive, own_row * cap + rank, slots)
    placing = lax.broadcasted_iota(I32, (slots, tok), 0) == slot
    place_ref[...] = jnp.where(placing, 1.0, 0.0).astype(BF16)
    position = lax.broadcasted_iota(I32, (tok, HD), 0) + meta_in[1:2, :HD]
    angle = position.astype(F32) * inverse[...]
    cos_ref[...] = jnp.cos(angle)
    front = lax.broadcasted_iota(I32, (tok, HD), 1) < HD // 2
    sine = jnp.sin(angle)
    sin_ref[...] = jnp.where(front, -sine, sine)

    for k in range(n_tensor):
        remote(ssq_out, ssq_in.at[k], ssq_sem, k, (after, dp, ten)).wait_recv()
    sum_sq = ssq_in[0]
    for k in range(1, n_tensor):
        sum_sq = sum_sq + ssq_in[k]
    scale = lax.rsqrt(sum_sq / d_model + EPSILON)
    scale_ref[...] = jnp.broadcast_to(scale, (HD, tok)).T

    def normed(at, wide):
        pieces = []
        for k in range(at, at + wide, HD):
            piece = rows[:, k : k + HD].astype(F32) * gain[:, k : k + HD] * scale_ref[...]
            pieces.append(piece.astype(BF16))
        return jnp.concatenate(pieces, axis=1)

    for j, (at, wide) in enumerate(chunks[:-1]):
        shifts[j].wait_recv()
        take_w[j].wait()
        activation = normed(at, wide)
        for n in range(0, total.shape[1], 256):
            product = dot(activation, w_vmem[at : at + wide, n : n + 256])
            total[:, n : n + 256] = product if j == 0 else total[:, n : n + 256] + product

    at, wide = chunks[-1]
    shifts[-1].wait_recv()
    take_w[-1].wait()
    activation = normed(at, wide)
    for n in range(n_ring):
        cols = pl.ds(pl.multiple_of((n * 2 + 1 - core) * 256, 256), 256)
        done = (total[:, cols] + dot(activation, w_vmem[at : at + wide, cols])).astype(BF16)
        pair_out[0, n] = done[:, :HD]
        pair_out[1, n] = done[:, HD:]
    to_pair = [remote(pair_out.at[g], pair_in.at[g], pair_sem, g, sibling) for g in range(2)]
    to_pair[0].start()
    to_pair[1].start()
    for n in range(n_ring):
        cols = pl.ds(pl.multiple_of((n * 2 + core) * 256, 256), 256)
        total[:, cols] += dot(activation, w_vmem[at : at + wide, cols])

    top, low = slice(0, half), slice(half, tok)

    def chip_sum(g, there):
        there = there % n_ring
        cols = pl.ds(pl.multiple_of((there * 2 + core) * 256 + g * HD, HD), HD)
        return total[:, cols] + pair_in[g, there].astype(F32)

    def hop(g, i, device):
        return remote(hop_out.at[g, i], hop_in.at[g, i], hop_sem, (g, i), device)

    for g in range(2):
        to_pair[g].wait_recv()
        across = chip_sum(g, ring + 2)
        hop_out[g, 0] = across[top].astype(BF16)
        hop_out[g, 1] = across[low].astype(BF16)
        hop(g, 0, right).start()
        hop(g, 1, left).start()
        to_right = chip_sum(g, ring + 1)
        hop_out[g, 2] = to_right[low].astype(BF16)
        hop(g, 2, right).start()
        late_ref[g, 0] = to_right[top]
        to_left = chip_sum(g, ring + n_ring - 1)
        hop_out[g, 3] = to_left[top].astype(BF16)
        hop(g, 3, left).start()
        late_ref[g, 1] = to_left[low]
    for g in range(2):
        hop(g, 0, right).wait_recv()
        hop_out[g, 4] = (late_ref[g, 0] + hop_in[g, 0].astype(F32)).astype(BF16)
        hop(g, 4, right).start()
        hop(g, 1, left).wait_recv()
        hop_out[g, 5] = (late_ref[g, 1] + hop_in[g, 1].astype(F32)).astype(BF16)
        hop(g, 5, left).start()

    keeps, routes = [], []
    for g in range(2):
        mine = chip_sum(g, ring)
        hop(g, 2, right).wait_recv()
        hop(g, 3, left).wait_recv()
        hop(g, 4, right).wait_recv()
        hop(g, 5, left).wait_recv()
        upper = mine[top] + hop_in[g, 4].astype(F32) + hop_in[g, 3].astype(F32)
        lower = mine[low] + hop_in[g, 2].astype(F32) + hop_in[g, 5].astype(F32)
        finished = jnp.concatenate([upper, lower], axis=0)
        if g == 0:
            finished = finished * cos_ref[...] + pltpu.roll(finished, HD // 2, 1) * sin_ref[...]
        packed[g] = dot(place_ref[...], finished.astype(BF16)).astype(BF16)
        cols = pl.ds(g * HD, HD)

        def slot_rows(group):
            return pl.ds(pl.multiple_of(group * cap, 16), cap)

        for k in sorted(range(1, n_dp), key=lambda k: -min(k, n_dp - k)):
            peer = (dp + k) % n_dp
            routes.append(
                remote(
                    packed.at[g, slot_rows(peer)],
                    out.at[0, 0, slot_rows(dp), cols],
                    route_sem,
                    (g, k),
                    (sec, peer, ten),
                )
            )
            routes[-1].start()
        keeps.append(
            pltpu.make_async_copy(
                packed.at[g, slot_rows(dp)], out.at[0, 0, slot_rows(dp), cols], keep_sem.at[g]
            )
        )
        keeps[-1].start()

    for copy in routes:
        copy.wait_recv()
    for copy in [*shifts, send_meta, *send_ssq, *to_pair, *routes]:
        copy.wait_send()
    for g in range(2):
        for i in range(6):
            hop(g, i, right).wait_send()
    for copy in keeps:
        copy.wait()


def per_device(sizes, hidden, owner, start, live, norm_gain, w_kv):
    n_section, n_dp, n_tensor, d_model = sizes
    tok, width = hidden.shape[2:]
    columns = w_kv.shape[2]
    slots = (3 * tok // (2 * n_dp)) * n_dp
    local_cols = columns // n_tensor
    exponent = np.arange(HD // 2, dtype=np.float32) * np.float32(2.0) / np.float32(HD)
    inverse = np.power(np.float32(ROPE_BASE), -exponent).astype(np.float32)
    inverse = jnp.asarray(np.concatenate([inverse, inverse])[None, :])
    n_chunks = len(feature_chunks(width))
    vmem, smem, anywhere = (
        pl.BlockSpec(memory_space=pltpu.VMEM),
        pl.BlockSpec(memory_space=pltpu.SMEM),
        pl.BlockSpec(memory_space=pl.ANY),
    )
    half = tok // 2
    n_ring = n_tensor // 2
    dma = pltpu.SemaphoreType.DMA
    return pl.pallas_call(
        functools.partial(kernel, sizes),
        out_shape=jax.ShapeDtypeStruct((1, 1, slots, local_cols), BF16),
        in_specs=[anywhere, vmem, smem, smem, vmem, vmem, anywhere],
        out_specs=anywhere,
        scratch_shapes=[
            pltpu.VMEM((tok, width), BF16),
            pltpu.VMEM((tok, width), BF16),
            pltpu.VMEM((width, columns), BF16),
            pltpu.VMEM((tok, columns), F32),
            pltpu.VMEM((1, tok), F32),
            pltpu.VMEM((n_tensor, 1, tok), F32),
            pltpu.VMEM((8, tok), I32),
            pltpu.VMEM((8, tok), I32),
            pltpu.VMEM((tok, HD), F32),
            pltpu.VMEM((tok, HD), F32),
            pltpu.VMEM((tok, HD), F32),
            pltpu.VMEM((slots, tok), BF16),
            pltpu.VMEM((2, n_ring, tok, HD), BF16),
            pltpu.VMEM((2, n_ring, tok, HD), BF16),
            pltpu.VMEM((2, 6, half, HD), BF16),
            pltpu.VMEM((2, 6, half, HD), BF16),
            pltpu.VMEM((2, 2, half, HD), F32),
            pltpu.VMEM((2, slots, HD), BF16),
            dma((1 + n_chunks,)),
            dma((2, n_chunks)),
            dma((2, n_tensor)),
            dma((2, 1)),
            dma((2, 2)),
            dma((2, 2, 6)),
            dma((2, 2, n_dp)),
            dma((2,)),
        ],
        compiler_params=pltpu.CompilerParams(
            collective_id=0, has_side_effects=True, vmem_limit_bytes=32 * 2**20
        ),
        cost_estimate=pl.CostEstimate(
            flops=2 * tok * width * columns,
            bytes_accessed=2 * width * (columns + 2 * tok),
            transcendentals=2 * tok * HD,
        ),
    )(hidden, owner.reshape(1, tok), start, live, norm_gain, inverse, w_kv)


def solution(mesh):
    sizes = (mesh.shape["section"], mesh.shape["dp"], mesh.shape["tensor"])
    in_specs = (
        P("section", "dp", None, "tensor"),
        P("section", "dp", None, None),
        P("section", "dp"),
        P("section", "dp"),
        P("section", "tensor"),
        P("section", "tensor", None),
    )
    out_specs = P("section", "dp", None, "tensor")

    def run(hidden, owner, start, live, norm_gain, w_kv):
        body = functools.partial(per_device, (*sizes, hidden.shape[3]))
        return jax.shard_map(
            body, mesh=mesh, in_specs=in_specs, out_specs=out_specs, check_vma=False
        )(hidden, owner, start, live, norm_gain, w_kv)

    return run
```

time: 193 us -> 75.7 us (0.39)
  the two profiles are of different devices: /device:TPU:8 before, /device:TPU:32 now
where the time goes in v1:
time: 75.7 us; the launch traced here: 75.4 us
  Pallas kernels  66.7 us (88%)
  local copies, waits for them, and re-layouts  7.31 us (10%)
  between operations  1.32 us (2%)
    pallas_call x1, Pallas kernels, per_device(): pl.pallas_call(functools.partial(kernel, sizes), out_shape=jax.ShapeDtype...  66.7 us
    unnamed x11, local copies, waits for them, and re-layouts  7.31 us

profile of v1, /device:TPU:32, one launch (start us, length us, event | category | flops | bytes accessed | tf_op | source)
XLA Modules:
  0.0 75.4 jit_solution(1573984744676483740)
XLA Ops:
  1.3 0.0 copy-start
  1.3 3.4 %copy-done = bf16[1,2048,2048]{2,1,0:T(8,128)(2,1)S(1)} copy-done((bf16[1,2048,2048]{2,1,0:T(8,128)(2,1)S(1)}, bf16[1,2048,2048]{2,1,0:T(8,128)(2,1)}, u32[]{:S(2)}) %copy-start) | copy-done | bytes 8388632
  4.7 0.0 copy-start.1
  4.7 1.2 %copy-done.1 = bf16[1,1,256,2048]{3,2,1,0:T(8,128)(2,1)S(1)} copy-done((bf16[1,1,256,2048]{3,2,1,0:T(8,128)(2,1)S(1)}, bf16[1,1,256,2048]{3,2,1,0:T(8,128)(2,1)}, u32[]{:S(2)}) %copy-start.1) | copy-done | bytes 1048600
  5.9 0.0 copy-start.2
  5.9 0.7 copy-done.2
  6.6 0.0 copy-start.3
  6.6 0.7 copy-done.3
  7.3 0.0 copy-start.4
  7.3 0.7 copy-done.4
  7.9 66.7 %shard_map.73 = bf16[1,1,384,256]{3,2,1,0:T(8,128)(2,1)S(1)} custom-call(bf16[1,1,256,2048]{3,2,1,0:T(8,128)(2,1)S(1)} %copy-done.1, s32[1,256]{1,0:T(1,128)S(1)} %bitcast.1, s32[1,1]{1,0:T(1,128)S(6)} %copy.9.start, s32[1,1]{1,0:T(1,128)S(6)} %copy.10.live, f32[1,2048]{1,0:T(1,128)S(1)} %copy-done.2, f32[1,128]{1,0:T(1,128)S(1)} %copy-done.4, ...), custom_call_target="tpu_custom_call" | custom-call | flops 2147483648 | bytes 10485760 | tf_op jit(solution)/shard_map/pallas_call | solution.py:293
  74.7 0.7 copy.11
Async XLA Ops:
  1.3 3.4 %copy-start = (bf16[1,2048,2048]{2,1,0:T(8,128)(2,1)S(1)}, bf16[1,2048,2048]{2,1,0:T(8,128)(2,1)}, u32[]{:S(2)}) copy-start(bf16[1,2048,2048]{2,1,0:T(8,128)(2,1)} %weight.1) | copy-start | bytes 25165828
  4.7 1.2 %copy-start.1 = (bf16[1,1,256,2048]{3,2,1,0:T(8,128)(2,1)S(1)}, bf16[1,1,256,2048]{3,2,1,0:T(8,128)(2,1)}, u32[]{:S(2)}) copy-start(bf16[1,1,256,2048]{3,2,1,0:T(8,128)(2,1)} %hidden.1) | copy-start | bytes 3145732
  5.9 0.7 copy-start.2
  6.6 0.7 copy-start.3
  7.3 0.7 copy-start.4

commit v2 on v1

v2 whole, which is shorter than its diff:
```python
import functools

import jax
import jax.numpy as jnp
import numpy as np
from jax import lax
from jax.experimental import pallas as pl
from jax.experimental.pallas import tpu as pltpu
from jax.sharding import PartitionSpec as P

HD = 128
EPSILON = 1e-05
ROPE_BASE = 500000.0
F32 = jnp.float32
BF16 = jnp.bfloat16
I32 = jnp.int32


GROUPS = ((256, 8),)
LAST_COLUMNS = 2


def units_of(groups, columns):
    units = [(q, 0, columns) for q in range(len(groups) - 1)]
    wide = columns // LAST_COLUMNS
    return units + [(len(groups) - 1, i * wide, wide) for i in range(LAST_COLUMNS)]


def pieces_of(groups, width):
    pieces, row = [], 0
    for q, (count, cuts) in enumerate(groups):
        wide = width // cuts
        pieces += [(q, row, count, i * wide, wide) for i in range(cuts)]
        row += count
    return pieces


def dot(a, b):
    return jnp.dot(a, b, preferred_element_type=F32)


def kernel(
    sizes,
    hidden,
    owner,
    start,
    live,
    gain,
    inverse,
    weight,
    out,
    own_rows,
    owner_vmem,
    gain_vmem,
    inverse_vmem,
    rows,
    w_vmem,
    total,
    ssq_out,
    ssq_in,
    meta_out,
    meta_in,
    scale_ref,
    cos_ref,
    sin_ref,
    place_ref,
    pair_out,
    pair_in,
    hop_out,
    hop_in,
    late_ref,
    slot_total,
    packed,
    local_sem,
    shift_sem,
    ssq_sem,
    meta_sem,
    pair_sem,
    hop_sem,
    route_sem,
    keep_sem,
):
    n_section, n_dp, n_tensor, d_model = sizes
    n_ring = n_tensor // 2
    tok, width = own_rows.shape
    slots, columns = packed.shape
    cap = slots // n_dp
    pieces = pieces_of(GROUPS, width)
    units = units_of(GROUPS, columns)
    first_row = [sum(count for count, _ in GROUPS[:q]) for q in range(len(GROUPS))]
    sec, dp, ten = lax.axis_index("section"), lax.axis_index("dp"), lax.axis_index("tensor")
    ring, core = ten // 2, ten % 2
    after = (sec + 1) % n_section
    before = (sec + n_section - 1) % n_section
    sends, takes = sec < n_section - 1, sec > 0
    sibling = (sec, dp, ring * 2 + 1 - core)
    right = (sec, dp, ((ring + 1) % n_ring) * 2 + core)
    left = (sec, dp, ((ring + n_ring - 1) % n_ring) * 2 + core)
    peers = [(sec, (dp + k) % n_dp, ten) for k in range(1, n_dp)]

    def remote(src, dst, sems, index, device, arrive=None):
        index = index if isinstance(index, tuple) else (index,)
        arrive = index if arrive is None else arrive
        return pltpu.make_async_remote_copy(
            src_ref=src,
            dst_ref=dst,
            send_sem=sems.at[(0, *index)],
            recv_sem=sems.at[(1, *arrive)],
            device_id=device,
            device_id_type=pl.DeviceIdType.MESH,
        )

    def shift(i):
        _, row, count, at, wide = pieces[i]
        here = (pl.ds(row, count), pl.ds(at, wide))
        return remote(hidden.at[(0, 0, *here)], rows.at[here], shift_sem, i, (after, dp, ten))

    def send_meta():
        return remote(meta_out, meta_in, meta_sem, 0, (after, dp, ten))

    def send_ssq(k):
        return remote(ssq_out, ssq_in.at[ten], ssq_sem, k, (after, dp, k), (ten,))

    def take(i):
        pairs = [(owner, owner_vmem), (hidden.at[0, 0], own_rows), (gain, gain_vmem), (inverse, inverse_vmem)]
        pairs.append((weight.at[0], w_vmem))
        return pltpu.make_async_copy(*pairs[i], local_sem.at[i])

    barrier = pltpu.get_barrier_semaphore()

    def greet(devices):
        for device in devices:
            pl.semaphore_signal(
                barrier, inc=1, device_id=device, device_id_type=pl.DeviceIdType.MESH
            )

    @pl.when(takes)
    def _():
        greet([(before, dp, t) for t in range(n_tensor)])
        greet([sibling, right, left, *peers])

    @pl.when(sends)
    def _():
        take(0).start()
        take(1).start()

    @pl.when(takes)
    def _():
        for i in (2, 3, 4):
            take(i).start()

    @pl.when(sec == 0)
    def _():
        packed[...] = jnp.zeros_like(packed)
        pltpu.make_async_copy(packed, out.at[0, 0], keep_sem.at[0]).start()

    @pl.when(sends)
    def _():
        take(0).wait()
        row_id = lax.broadcasted_iota(I32, (8, tok), 0)
        meta_out[...] = jnp.where(
            row_id == 0, owner_vmem[...], jnp.where(row_id == 1, start[0, 0], live[0, 0])
        )

    within = 3 + len(peers)

    @pl.when(sends & takes)
    def _():
        pl.semaphore_wait(barrier, n_tensor + within)

    @pl.when(sec == 0)
    def _():
        pl.semaphore_wait(barrier, n_tensor)

    @pl.when(sec == n_section - 1)
    def _():
        pl.semaphore_wait(barrier, within)

    @pl.when(sends)
    def _():
        send_meta().start()
        shift(0).start()
        take(1).wait()
        squares = jnp.zeros((tok, HD), F32)
        for k in range(width // HD):
            piece = own_rows[:, k * HD : (k + 1) * HD].astype(F32)
            squares = squares + piece * piece
        ssq_out[...] = jnp.sum(squares.T, axis=0, keepdims=True)
        for k in range(n_tensor):
            send_ssq(k).start()
        for i in range(1, len(pieces)):
            shift(i).start()

    def prepare():
        send_meta().wait_recv()
        own_row = meta_in[0:1, :]
        alive = lax.broadcasted_iota(I32, (1, tok), 1) < meta_in[2:3, :]
        named = (lax.broadcasted_iota(I32, (16, tok), 0) == own_row) & alive
        named = jnp.where(named, 1.0, 0.0)
        row_at = lax.broadcasted_iota(I32, (tok, tok), 0)
        earlier = row_at < lax.broadcasted_iota(I32, (tok, tok), 1)
        ranks = dot(named.astype(BF16), jnp.where(earlier, 1.0, 0.0).astype(BF16))
        rank = jnp.sum(ranks * named, axis=0, keepdims=True).astype(I32)
        slot = jnp.where(alive, own_row * cap + rank, slots)
        placing = lax.broadcasted_iota(I32, (slots, tok), 0) == slot
        placing = jnp.where(placing, 1.0, 0.0).astype(BF16)
        for q, (count, _) in enumerate(GROUPS):
            place_ref[q, :, :count] = placing[:, first_row[q] : first_row[q] + count]
        position = lax.broadcasted_iota(I32, (tok, HD), 0) + meta_in[1:2, :HD]
        take(3).wait()
        take(2).wait()
        angle = position.astype(F32) * inverse_vmem[...]
        cos_ref[...] = jnp.cos(angle)
        front = lax.broadcasted_iota(I32, (tok, HD), 1) < HD // 2
        sine = jnp.sin(angle)
        sin_ref[...] = jnp.where(front, -sine, sine)
        for k in range(n_tensor):
            remote(ssq_out, ssq_in.at[k], ssq_sem, k, (after, dp, ten)).wait_recv()
        sum_sq = ssq_in[0]
        for k in range(1, n_tensor):
            sum_sq = sum_sq + ssq_in[k]
        scale = lax.rsqrt(sum_sq / d_model + EPSILON)
        scale_ref[...] = jnp.broadcast_to(scale, (HD, tok)).T

    def normed(row, count, at, wide):
        here = slice(row, row + count)
        scale = scale_ref[here]
        parts = []
        for k in range(at, at + wide, HD):
            part = rows[here, k : k + HD].astype(F32) * gain_vmem[:, k : k + HD] * scale
            parts.append(part.astype(BF16))
        return jnp.concatenate(parts, axis=1)

    def pair(q):
        here = pl.ds(first_row[q], GROUPS[q][0])
        return remote(pair_out.at[:, here], pair_in.at[:, here], pair_sem, q, sibling)

    def project(q):
        mine = [(i, p) for i, p in enumerate(pieces) if p[0] == q]
        for i, (_, row, count, at, wide) in mine:
            here = slice(row, row + count)
            shift(i).wait_recv()
            if i == 0:
                take(4).wait()
            activation = normed(row, count, at, wide)
            if i != mine[-1][0]:
                for n in range(0, total.shape[1], columns):
                    cols = slice(n, n + columns)
                    product = dot(activation, w_vmem[at : at + wide, cols])
                    total[here, cols] = product if at == 0 else total[here, cols] + product
                continue
            for side in (1 - core, core):
                for n in range(n_ring):
                    cols = pl.ds(pl.multiple_of((n * 2 + side) * columns, columns), columns)
                    product = dot(activation, w_vmem[at : at + wide, cols])
                    if at:
                        product = total[here, cols] + product
                    if side is core:
                        total[here, cols] = product
                    else:
                        pair_out[n, here] = product.astype(BF16)
                if side is not core:
                    pair(q).start()

    def rows_of(q):
        row, count = first_row[q], GROUPS[q][0]
        return row, row + count // 2, row + count

    def chip_sum(u, there, first, last):
        _, at, wide = units[u]
        there = there % n_ring
        cols = pl.ds(pl.multiple_of((there * 2 + core) * columns + at, HD), wide)
        here = slice(first, last)
        return total[here, cols] + pair_in[there, here, at : at + wide].astype(F32)

    def view(u):
        q, at, wide = units[u]
        return slice(first_row[q] // 2, (first_row[q] + GROUPS[q][0]) // 2), slice(at, at + wide)

    def hop(u, i, device):
        r, c = view(u)
        here = (i, pl.ds(r.start, r.stop - r.start), pl.ds(c.start, c.stop - c.start))
        return remote(hop_out.at[here], hop_in.at[here], hop_sem, (u, i), device)

    def across(u):
        a, b, c = rows_of(units[u][0])
        r, cols = view(u)
        hop_out[0, r, cols] = chip_sum(u, ring + 2, a, b).astype(BF16)
        hop(u, 0, right).start()
        hop_out[1, r, cols] = chip_sum(u, ring + 2, b, c).astype(BF16)
        hop(u, 1, left).start()
        hop_out[2, r, cols] = chip_sum(u, ring + 1, b, c).astype(BF16)
        hop(u, 2, right).start()
        hop_out[3, r, cols] = chip_sum(u, ring + n_ring - 1, a, b).astype(BF16)
        hop(u, 3, left).start()
        late_ref[0, r, cols] = chip_sum(u, ring + 1, a, b)
        late_ref[1, r, cols] = chip_sum(u, ring + n_ring - 1, b, c)

    def relay(u):
        r, cols = view(u)
        for side, device in ((0, right), (1, left)):
            hop(u, side, device).wait_recv()
            both = late_ref[side, r, cols] + hop_in[side, r, cols].astype(F32)
            hop_out[4 + side, r, cols] = both.astype(BF16)
            hop(u, 4 + side, device).start()

    def slot_rows(group):
        return pl.ds(pl.multiple_of(group * cap, 16), cap)

    def route(g, k):
        cols = pl.ds(g * HD, HD)
        peer = (dp + k) % n_dp
        return remote(
            packed.at[slot_rows(peer), cols],
            out.at[0, 0, slot_rows(dp), cols],
            route_sem,
            (g, k),
            (sec, peer, ten),
        )

    def keep(g):
        cols = pl.ds(g * HD, HD)
        return pltpu.make_async_copy(
            packed.at[slot_rows(dp), cols], out.at[0, 0, slot_rows(dp), cols], keep_sem.at[g]
        )

    def finish(u):
        q, at, wide = units[u]
        a, b, c = rows_of(q)
        r, cols = view(u)
        mine = chip_sum(u, ring, a, c)
        for i in (2, 3, 4, 5):
            hop(u, i, right).wait_recv()
        upper = hop_in[4, r, cols].astype(F32) + hop_in[3, r, cols].astype(F32)
        lower = hop_in[2, r, cols].astype(F32) + hop_in[5, r, cols].astype(F32)
        rows_done = mine + jnp.concatenate([upper, lower], axis=0)
        for k in range(0, wide, HD):
            part = rows_done[:, k : k + HD]
            g = (at + k) // HD
            if g % 2 == 0:
                part = part * cos_ref[a:c] + pltpu.roll(part, HD // 2, 1) * sin_ref[a:c]
            put = dot(place_ref[q, :, : c - a], part.astype(BF16))
            there = slice(g * HD, (g + 1) * HD)
            if q:
                put = slot_total[:, there] + put
            if q < len(GROUPS) - 1:
                slot_total[:, there] = put
                continue
            packed[:, there] = put.astype(BF16)
            for k in routed:
                route(g, k).start()
            keep(g).start()

    routed = sorted(range(1, n_dp), key=lambda k: -min(k, n_dp - k))

    @pl.when(takes)
    def _():
        prepare()
        for q in range(len(GROUPS)):
            project(q)
            now = [u for u, unit in enumerate(units) if unit[0] == q]
            pair(q).wait_recv()
            for u in now:
                across(u)
            for u, unit in enumerate(units):
                if unit[0] == q - 1:
                    finish(u)
            for u in now:
                relay(u)
        for u in now:
            finish(u)
        for g in range(columns // HD):
            for k in routed:
                route(g, k).wait_recv()
        for g in range(columns // HD):
            for k in routed:
                route(g, k).wait_send()
            keep(g).wait()
        for q in range(len(GROUPS)):
            pair(q).wait_send()
        for u in range(len(units)):
            for i in range(6):
                hop(u, i, right).wait_send()

    @pl.when(sends)
    def _():
        for i in range(len(pieces)):
            shift(i).wait_send()
        send_meta().wait_send()
        for k in range(n_tensor):
            send_ssq(k).wait_send()

    @pl.when(sec == 0)
    def _():
        pltpu.make_async_copy(packed, out.at[0, 0], keep_sem.at[0]).wait()


def per_device(sizes, hidden, owner, start, live, norm_gain, w_kv):
    n_section, n_dp, n_tensor, d_model = sizes
    tok, width = hidden.shape[2:]
    columns = w_kv.shape[2]
    slots = (3 * tok // (2 * n_dp)) * n_dp
    local_cols = columns // n_tensor
    exponent = np.arange(HD // 2, dtype=np.float32) * np.float32(2.0) / np.float32(HD)
    inverse = np.power(np.float32(ROPE_BASE), -exponent).astype(np.float32)
    inverse = jnp.asarray(np.concatenate([inverse, inverse])[None, :])
    smem = pl.BlockSpec(memory_space=pltpu.SMEM)
    hbm = pl.BlockSpec(memory_space=pltpu.HBM)
    half = tok // 2
    n_ring = n_tensor // 2
    most = max(count for count, _ in GROUPS)
    n_units = len(units_of(GROUPS, local_cols))
    dma = pltpu.SemaphoreType.DMA
    return pl.pallas_call(
        functools.partial(kernel, sizes),
        out_shape=jax.ShapeDtypeStruct((1, 1, slots, local_cols), BF16),
        in_specs=[hbm, hbm, smem, smem, hbm, hbm, hbm],
        out_specs=hbm,
        scratch_shapes=[
            pltpu.VMEM((tok, width), BF16),
            pltpu.VMEM((1, tok), I32),
            pltpu.VMEM((1, width), F32),
            pltpu.VMEM((1, HD), F32),
            pltpu.VMEM((tok, width), BF16),
            pltpu.VMEM((width, columns), BF16),
            pltpu.VMEM((tok, columns), F32),
            pltpu.VMEM((1, tok), F32),
            pltpu.VMEM((n_tensor, 1, tok), F32),
            pltpu.VMEM((8, tok), I32),
            pltpu.VMEM((8, tok), I32),
            pltpu.VMEM((tok, HD), F32),
            pltpu.VMEM((tok, HD), F32),
            pltpu.VMEM((tok, HD), F32),
            pltpu.VMEM((len(GROUPS), slots, most), BF16),
            pltpu.VMEM((n_ring, tok, local_cols), BF16),
            pltpu.VMEM((n_ring, tok, local_cols), BF16),
            pltpu.VMEM((6, half, local_cols), BF16),
            pltpu.VMEM((6, half, local_cols), BF16),
            pltpu.VMEM((2, half, local_cols), F32),
            pltpu.VMEM((slots, local_cols), F32),
            pltpu.VMEM((slots, local_cols), BF16),
            dma((5,)),
            dma((2, len(pieces_of(GROUPS, width)))),
            dma((2, n_tensor)),
            dma((2, 1)),
            dma((2, len(GROUPS))),
            dma((2, n_units, 6)),
            dma((2, local_cols // HD, n_dp)),
            dma((local_cols // HD,)),
        ],
        compiler_params=pltpu.CompilerParams(
            collective_id=0, has_side_effects=True, vmem_limit_bytes=60 * 2**20
        ),
        cost_estimate=pl.CostEstimate(
            flops=2 * tok * width * columns,
            bytes_accessed=2 * width * (columns + 2 * tok),
            transcendentals=2 * tok * HD,
        ),
    )(hidden, owner.reshape(1, tok), start, live, norm_gain, inverse, w_kv)


def solution(mesh):
    sizes = (mesh.shape["section"], mesh.shape["dp"], mesh.shape["tensor"])
    in_specs = (
        P("section", "dp", None, "tensor"),
        P("section", "dp", None, None),
        P("section", "dp"),
        P("section", "dp"),
        P("section", "tensor"),
        P("section", "tensor", None),
    )
    out_specs = P("section", "dp", None, "tensor")

    def run(hidden, owner, start, live, norm_gain, w_kv):
        body = functools.partial(per_device, (*sizes, hidden.shape[3]))
        return jax.shard_map(
            body, mesh=mesh, in_specs=in_specs, out_specs=out_specs, check_vma=False
        )(hidden, owner, start, live, norm_gain, w_kv)

    return run
```

time: 75.7 us -> 58.6 us (0.77)
  the two profiles are of different devices: /device:TPU:32 before, /device:TPU:512 now
where the time goes in v2:
time: 58.6 us; the launch traced here: 58.4 us
  Pallas kernels  55.5 us (95%)
  local copies, waits for them, and re-layouts  1.62 us (3%)
  between operations  1.3 us (2%)
    pallas_call x1, Pallas kernels, per_device(): pl.pallas_call(functools.partial(kernel, sizes), out_shape=jax.ShapeDtype...  55.5 us
    unnamed x1, local copies, waits for them, and re-layouts  1.62 us

profile of v2, /device:TPU:512, one launch (start us, length us, event | category | flops | bytes accessed | tf_op | source)
XLA Modules:
  0.0 58.4 jit_solution(11967792025544369569)
XLA Ops:
  1.3 55.5 %shard_map.73 = bf16[1,1,384,256]{3,2,1,0:T(8,128)(2,1)} custom-call(bf16[1,1,256,2048]{3,2,1,0:T(8,128)(2,1)} %hidden.1, s32[1,256]{1,0:T(1,128)} %bitcast.1, s32[1,1]{1,0:T(1,128)S(6)} %copy.9.start, s32[1,1]{1,0:T(1,128)S(6)} %copy.10.live, f32[1,2048]{1,0:T(1,128)} %gain.1, f32[1,128]{1,0:T(1,128)} %constant.2.clone.inverse, bf16[1,2048,2048]{2,1,0:T(8,128)(2,1)} %weight.1), custom_call_target="tpu_custom_call" | custom-call | flops 2147483648 | bytes 10485760 | tf_op jit(solution)/shard_map/pallas_call | solution.py:414
  56.8 1.6 %copy.11 = bf16[1,1,384,256]{3,2,1,0:T(8,128)(2,1)} copy(bf16[1,1,384,256]{3,2,1,0:T(8,128)(2,1)} %shard_map.73) | data formatting | bytes 393216

commit v3 on v2

--- a/solution.py
+++ b/solution.py
@@ -16,23 +16,13 @@
 I32 = jnp.int32
 
 
-GROUPS = ((256, 8),)
-LAST_COLUMNS = 2
-
-
-def units_of(groups, columns):
-    units = [(q, 0, columns) for q in range(len(groups) - 1)]
-    wide = columns // LAST_COLUMNS
-    return units + [(len(groups) - 1, i * wide, wide) for i in range(LAST_COLUMNS)]
-
-
-def pieces_of(groups, width):
-    pieces, row = [], 0
-    for q, (count, cuts) in enumerate(groups):
-        wide = width // cuts
-        pieces += [(q, row, count, i * wide, wide) for i in range(cuts)]
-        row += count
-    return pieces
+PIECES = 8
+
+
+def feature_pieces(width):
+    count = min(PIECES, width // HD)
+    wide = width // count
+    return [(i * wide, wide) for i in range(count)]
 
 
 def dot(a, b):
@@ -69,7 +59,6 @@
     hop_out,
     hop_in,
     late_ref,
-    slot_total,
     packed,
     local_sem,
     shift_sem,
@@ -85,9 +74,8 @@
     tok, width = own_rows.shape
     slots, columns = packed.shape
     cap = slots // n_dp
-    pieces = pieces_of(GROUPS, width)
-    units = units_of(GROUPS, columns)
-    first_row = [sum(count for count, _ in GROUPS[:q]) for q in range(len(GROUPS))]
+    half = tok // 2
+    pieces = feature_pieces(width)
     sec, dp, ten = lax.axis_index("section"), lax.axis_index("dp"), lax.axis_index("tensor")
     ring, core = ten // 2, ten % 2
     after = (sec + 1) % n_section
@@ -111,8 +99,7 @@
         )
 
     def shift(i):
-        _, row, count, at, wide = pieces[i]
-        here = (pl.ds(row, count), pl.ds(at, wide))
+        here = (slice(None), pl.ds(*pieces[i]))
         return remote(hidden.at[(0, 0, *here)], rows.at[here], shift_sem, i, (after, dp, ten))
 
     def send_meta():
@@ -204,8 +191,7 @@
         slot = jnp.where(alive, own_row * cap + rank, slots)
         placing = lax.broadcasted_iota(I32, (slots, tok), 0) == slot
         placing = jnp.where(placing, 1.0, 0.0).astype(BF16)
-        for q, (count, _) in enumerate(GROUPS):
-            place_ref[q, :, :count] = placing[:, first_row[q] : first_row[q] + count]
+        place_ref[...] = placing
         position = lax.broadcasted_iota(I32, (tok, HD), 0) + meta_in[1:2, :HD]
         take(3).wait()
         take(2).wait()
@@ -222,87 +208,92 @@
         scale = lax.rsqrt(sum_sq / d_model + EPSILON)
         scale_ref[...] = jnp.broadcast_to(scale, (HD, tok)).T
 
-    def normed(row, count, at, wide):
-        here = slice(row, row + count)
-        scale = scale_ref[here]
+    def normed(at, wide):
+        scale = scale_ref[...]
         parts = []
         for k in range(at, at + wide, HD):
-            part = rows[here, k : k + HD].astype(F32) * gain_vmem[:, k : k + HD] * scale
+            part = rows[:, k : k + HD].astype(F32) * gain_vmem[:, k : k + HD] * scale
             parts.append(part.astype(BF16))
         return jnp.concatenate(parts, axis=1)
 
-    def pair(q):
-        here = pl.ds(first_row[q], GROUPS[q][0])
-        return remote(pair_out.at[:, here], pair_in.at[:, here], pair_sem, q, sibling)
-
-    def project(q):
-        mine = [(i, p) for i, p in enumerate(pieces) if p[0] == q]
-        for i, (_, row, count, at, wide) in mine:
-            here = slice(row, row + count)
+    turns = (2, 1, n_ring - 1, 0)
+
+    def chip(turn):
+        return (ring + turn) % n_ring
+
+    def cols_of(turn, side):
+        return pl.ds(pl.multiple_of((chip(turn) * 2 + side) * columns, columns), columns)
+
+    def pair(j):
+        here = chip(turns[j])
+        return remote(pair_out.at[here], pair_in.at[here], pair_sem, j, sibling)
+
+    def project():
+        for i, (at, wide) in enumerate(pieces[:-1]):
             shift(i).wait_recv()
             if i == 0:
                 take(4).wait()
-            activation = normed(row, count, at, wide)
-            if i != mine[-1][0]:
-                for n in range(0, total.shape[1], columns):
-                    cols = slice(n, n + columns)
-                    product = dot(activation, w_vmem[at : at + wide, cols])
-                    total[here, cols] = product if at == 0 else total[here, cols] + product
-                continue
-            for side in (1 - core, core):
-                for n in range(n_ring):
-                    cols = pl.ds(pl.multiple_of((n * 2 + side) * columns, columns), columns)
-                    product = dot(activation, w_vmem[at : at + wide, cols])
-                    if at:
-                        product = total[here, cols] + product
-                    if side is core:
-                        total[here, cols] = product
-                    else:
-                        pair_out[n, here] = product.astype(BF16)
-                if side is not core:
-                    pair(q).start()
-
-    def rows_of(q):
-        row, count = first_row[q], GROUPS[q][0]
-        return row, row + count // 2, row + count
-
-    def chip_sum(u, there, first, last):
-        _, at, wide = units[u]
-        there = there % n_ring
-        cols = pl.ds(pl.multiple_of((there * 2 + core) * columns + at, HD), wide)
-        here = slice(first, last)
-        return total[here, cols] + pair_in[there, here, at : at + wide].astype(F32)
-
-    def view(u):
-        q, at, wide = units[u]
-        return slice(first_row[q] // 2, (first_row[q] + GROUPS[q][0]) // 2), slice(at, at + wide)
-
-    def hop(u, i, device):
-        r, c = view(u)
-        here = (i, pl.ds(r.start, r.stop - r.start), pl.ds(c.start, c.stop - c.start))
-        return remote(hop_out.at[here], hop_in.at[here], hop_sem, (u, i), device)
-
-    def across(u):
-        a, b, c = rows_of(units[u][0])
-        r, cols = view(u)
-        hop_out[0, r, cols] = chip_sum(u, ring + 2, a, b).astype(BF16)
-        hop(u, 0, right).start()
-        hop_out[1, r, cols] = chip_sum(u, ring + 2, b, c).astype(BF16)
-        hop(u, 1, left).start()
-        hop_out[2, r, cols] = chip_sum(u, ring + 1, b, c).astype(BF16)
-        hop(u, 2, right).start()
-        hop_out[3, r, cols] = chip_sum(u, ring + n_ring - 1, a, b).astype(BF16)
-        hop(u, 3, left).start()
-        late_ref[0, r, cols] = chip_sum(u, ring + 1, a, b)
-        late_ref[1, r, cols] = chip_sum(u, ring + n_ring - 1, b, c)
-
-    def relay(u):
-        r, cols = view(u)
+            activation = normed(at, wide)
+            for n in range(0, total.shape[1], columns):
+                cols = slice(n, n + columns)
+                product = dot(activation, w_vmem[at : at + wide, cols])
+                total[:, cols] = total[:, cols] + product if at else product
+        at, wide = pieces[-1]
+        shift(len(pieces) - 1).wait_recv()
+        activation = normed(at, wide)
+        for j, turn in enumerate(turns):
+            cols = cols_of(turn, 1 - core)
+            done = total[:, cols] + dot(activation, w_vmem[at : at + wide, cols])
+            pair_out[chip(turn)] = done.astype(BF16)
+            pair(j).start()
+        for turn in turns:
+            cols = cols_of(turn, core)
+            total[:, cols] += dot(activation, w_vmem[at : at + wide, cols])
+
+    def chip_sum(turn, rows_from, rows_to, cols):
+        mine = total[rows_from:rows_to, cols_of(turn, core)]
+        theirs = pair_in[chip(turn), rows_from:rows_to].astype(F32)
+        return (mine + theirs)[:, cols]
+
+    everything, key_cols, value_cols = slice(0, columns), slice(0, HD), slice(HD, columns)
+    parts = (key_cols, value_cols)
+
+    def hop(g, i, device):
+        cols = everything if i < 2 else parts[g]
+        here = (i, slice(None), pl.ds(cols.start, cols.stop - cols.start))
+        return remote(hop_out.at[here], hop_in.at[here], hop_sem, (g, i), device)
+
+    def straight(g):
+        hop_out[2, :, parts[g]] = late_ref[2, :, parts[g]].astype(BF16)
+        hop(g, 2, right).start()
+        hop_out[3, :, parts[g]] = late_ref[3, :, parts[g]].astype(BF16)
+        hop(g, 3, left).start()
+
+    def relay(g):
         for side, device in ((0, right), (1, left)):
-            hop(u, side, device).wait_recv()
-            both = late_ref[side, r, cols] + hop_in[side, r, cols].astype(F32)
-            hop_out[4 + side, r, cols] = both.astype(BF16)
-            hop(u, 4 + side, device).start()
+            if g == 0:
+                hop(0, side, device).wait_recv()
+            both = late_ref[side, :, parts[g]] + hop_in[side, :, parts[g]].astype(F32)
+            hop_out[4 + side, :, parts[g]] = both.astype(BF16)
+            hop(g, 4 + side, device).start()
+
+    def ring_sums():
+        pair(0).wait_recv()
+        hop_out[0] = chip_sum(2, 0, half, everything).astype(BF16)
+        hop(0, 0, right).start()
+        hop_out[1] = chip_sum(2, half, tok, everything).astype(BF16)
+        hop(0, 1, left).start()
+        pair(1).wait_recv()
+        late_ref[0] = chip_sum(1, 0, half, everything)
+        late_ref[2] = chip_sum(1, half, tok, everything)
+        pair(2).wait_recv()
+        late_ref[1] = chip_sum(n_ring - 1, half, tok, everything)
+        late_ref[3] = chip_sum(n_ring - 1, 0, half, everything)
+        straight(0)
+        relay(0)
+        straight(1)
+        relay(1)
+        pair(3).wait_recv()
 
     def slot_rows(group):
         return pl.ds(pl.multiple_of(group * cap, 16), cap)
@@ -324,63 +315,43 @@
             packed.at[slot_rows(dp), cols], out.at[0, 0, slot_rows(dp), cols], keep_sem.at[g]
         )
 
-    def finish(u):
-        q, at, wide = units[u]
-        a, b, c = rows_of(q)
-        r, cols = view(u)
-        mine = chip_sum(u, ring, a, c)
+    routed = sorted(range(1, n_dp), key=lambda k: -min(k, n_dp - k))
+
+    def finish(g):
+        cols = parts[g]
+        mine = chip_sum(0, 0, tok, cols)
         for i in (2, 3, 4, 5):
-            hop(u, i, right).wait_recv()
-        upper = hop_in[4, r, cols].astype(F32) + hop_in[3, r, cols].astype(F32)
-        lower = hop_in[2, r, cols].astype(F32) + hop_in[5, r, cols].astype(F32)
-        rows_done = mine + jnp.concatenate([upper, lower], axis=0)
-        for k in range(0, wide, HD):
-            part = rows_done[:, k : k + HD]
-            g = (at + k) // HD
-            if g % 2 == 0:
-                part = part * cos_ref[a:c] + pltpu.roll(part, HD // 2, 1) * sin_ref[a:c]
-            put = dot(place_ref[q, :, : c - a], part.astype(BF16))
-            there = slice(g * HD, (g + 1) * HD)
-            if q:
-                put = slot_total[:, there] + put
-            if q < len(GROUPS) - 1:
-                slot_total[:, there] = put
-                continue
-            packed[:, there] = put.astype(BF16)
-            for k in routed:
-                route(g, k).start()
-            keep(g).start()
-
-    routed = sorted(range(1, n_dp), key=lambda k: -min(k, n_dp - k))
+            hop(g, i, right).wait_recv()
+        upper = hop_in[4, :, cols].astype(F32) + hop_in[3, :, cols].astype(F32)
+        lower = hop_in[2, :, cols].astype(F32) + hop_in[5, :, cols].astype(F32)
+        done = mine + jnp.concatenate([upper, lower], axis=0)
+        if g == 0:
+            done = done * cos_ref[...] + pltpu.roll(done, HD // 2, 1) * sin_ref[...]
+        packed[:, cols] = dot(place_ref[...], done.astype(BF16)).astype(BF16)
+        for k in routed:
+            route(g, k).start()
+        keep(g).start()
 
     @pl.when(takes)
     def _():
         prepare()
-        for q in range(len(GROUPS)):
-            project(q)
-            now = [u for u, unit in enumerate(units) if unit[0] == q]
-            pair(q).wait_recv()
-            for u in now:
-                across(u)
-            for u, unit in enumerate(units):
-                if unit[0] == q - 1:
-                    finish(u)
-            for u in now:
-                relay(u)
-        for u in now:
-            finish(u)
-        for g in range(columns // HD):
+        project()
+        ring_sums()
+        finish(0)
+        finish(1)
+        for g in range(2):
             for k in routed:
                 route(g, k).wait_recv()
-        for g in range(columns // HD):
+        for g in range(2):
             for k in routed:
                 route(g, k).wait_send()
             keep(g).wait()
-        for q in range(len(GROUPS)):
-            pair(q).wait_send()
-        for u in range(len(units)):
-            for i in range(6):
-                hop(u, i, right).wait_send()
+            for i in range(2, 6):
+                hop(g, i, right).wait_send()
+        for j in range(len(turns)):
+            pair(j).wait_send()
+        hop(0, 0, right).wait_send()
+        hop(0, 1, left).wait_send()
 
     @pl.when(sends)
     def _():
@@ -393,6 +364,10 @@
     @pl.when(sec == 0)
     def _():
         pltpu.make_async_copy(packed, out.at[0, 0], keep_sem.at[0]).wait()
+
+
+def pinned(x):
+    return pltpu.with_memory_space_constraint(x, pltpu.HBM)
 
 
 def per_device(sizes, hidden, owner, start, live, norm_gain, w_kv):
@@ -408,8 +383,6 @@
     hbm = pl.BlockSpec(memory_space=pltpu.HBM)
     half = tok // 2
     n_ring = n_tensor // 2
-    most = max(count for count, _ in GROUPS)
-    n_units = len(units_of(GROUPS, local_cols))
     dma = pltpu.SemaphoreType.DMA
     return pl.pallas_call(
         functools.partial(kernel, sizes),
@@ -431,32 +404,31 @@
             pltpu.VMEM((tok, HD), F32),
             pltpu.VMEM((tok, HD), F32),
             pltpu.VMEM((tok, HD), F32),
-            pltpu.VMEM((len(GROUPS), slots, most), BF16),
+            pltpu.VMEM((slots, tok), BF16),
             pltpu.VMEM((n_ring, tok, local_cols), BF16),
             pltpu.VMEM((n_ring, tok, local_cols), BF16),
             pltpu.VMEM((6, half, local_cols), BF16),
             pltpu.VMEM((6, half, local_cols), BF16),
-            pltpu.VMEM((2, half, local_cols), F32),
-            pltpu.VMEM((slots, local_cols), F32),
+            pltpu.VMEM((4, half, local_cols), F32),
             pltpu.VMEM((slots, local_cols), BF16),
             dma((5,)),
-            dma((2, len(pieces_of(GROUPS, width)))),
+            dma((2, len(feature_pieces(width)))),
             dma((2, n_tensor)),
             dma((2, 1)),
-            dma((2, len(GROUPS))),
-            dma((2, n_units, 6)),
-            dma((2, local_cols // HD, n_dp)),
-            dma((local_cols // HD,)),
+            dma((2, n_ring)),
+            dma((2, 2, 6)),
+            dma((2, 2, n_dp)),
+            dma((2,)),
         ],
         compiler_params=pltpu.CompilerParams(
-            collective_id=0, has_side_effects=True, vmem_limit_bytes=60 * 2**20
+            collective_id=0, has_side_effects=True, vmem_limit_bytes=32 * 2**20
         ),
         cost_estimate=pl.CostEstimate(
             flops=2 * tok * width * columns,
             bytes_accessed=2 * width * (columns + 2 * tok),
             transcendentals=2 * tok * HD,
         ),
-    )(hidden, owner.reshape(1, tok), start, live, norm_gain, inverse, w_kv)
+    )(pinned(hidden), pinned(owner.reshape(1, tok)), start, live, pinned(norm_gain), pinned(inverse), pinned(w_kv))
 
 
 def solution(mesh):

time: 58.6 us -> 57.9 us (0.988)
  local copies, waits for them, and re-layouts: 1.62 us -> 0.68 us
    unnamed x1, local copies, waits for them, and re-layouts: 1.62 us -> 0.68 us
where the time goes in v3:
time: 57.9 us; the launch traced here: 57.7 us
  Pallas kernels  55.7 us (96%)
  between operations  1.3 us (2%)
  local copies, waits for them, and re-layouts  0.68 us (1%)
    pallas_call x1, Pallas kernels, per_device(): pl.pallas_call(functools.partial(kernel, sizes), out_shape=jax.ShapeDtype...  55.7 us

profile of v3, /device:TPU:512, one launch (start us, length us, event | category | flops | bytes accessed | tf_op | source)
XLA Modules:
  0.0 57.7 jit_solution(5231512964479944050)
XLA Ops:
  1.3 55.7 %shard_map.73 = bf16[1,1,384,256]{3,2,1,0:T(8,128)(2,1)S(1)} custom-call(bf16[1,1,256,2048]{3,2,1,0:T(8,128)(2,1)} %hidden.1, s32[1,256]{1,0:T(1,128)} %bitcast.1, s32[1,1]{1,0:T(1,128)S(6)} %copy.9.start, s32[1,1]{1,0:T(1,128)S(6)} %copy.10.live, f32[1,2048]{1,0:T(1,128)} %gain.1, f32[1,128]{1,0:T(1,128)} %constant.2.clone.inverse, ...), custom_call_target="tpu_custom_call" | custom-call | flops 2147483648 | bytes 10485760 | tf_op jit(solution)/shard_map/pallas_call | solution.py:387
  57.0 0.7 %copy.11 = bf16[1,1,384,256]{3,2,1,0:T(8,128)(2,1)} copy(bf16[1,1,384,256]{3,2,1,0:T(8,128)(2,1)S(1)} %shard_map.73) | data formatting | bytes 393216

commit v4 on v3

--- a/solution.py
+++ b/solution.py
@@ -259,8 +259,7 @@
     parts = (key_cols, value_cols)
 
     def hop(g, i, device):
-        cols = everything if i < 2 else parts[g]
-        here = (i, slice(None), pl.ds(cols.start, cols.stop - cols.start))
+        here = (i, slice(None), pl.ds(parts[g].start, HD))
         return remote(hop_out.at[here], hop_in.at[here], hop_sem, (g, i), device)
 
     def straight(g):
@@ -271,8 +270,7 @@
 
     def relay(g):
         for side, device in ((0, right), (1, left)):
-            if g == 0:
-                hop(0, side, device).wait_recv()
+            hop(g, side, device).wait_recv()
             both = late_ref[side, :, parts[g]] + hop_in[side, :, parts[g]].astype(F32)
             hop_out[4 + side, :, parts[g]] = both.astype(BF16)
             hop(g, 4 + side, device).start()
@@ -290,6 +288,8 @@
         late_ref[1] = chip_sum(n_ring - 1, half, tok, everything)
         late_ref[3] = chip_sum(n_ring - 1, 0, half, everything)
         straight(0)
+        hop(1, 0, right).start()
+        hop(1, 1, left).start()
         relay(0)
         straight(1)
         relay(1)
@@ -319,12 +319,15 @@
 
     def finish(g):
         cols = parts[g]
-        mine = chip_sum(0, 0, tok, cols)
-        for i in (2, 3, 4, 5):
-            hop(g, i, right).wait_recv()
-        upper = hop_in[4, :, cols].astype(F32) + hop_in[3, :, cols].astype(F32)
-        lower = hop_in[2, :, cols].astype(F32) + hop_in[5, :, cols].astype(F32)
-        done = mine + jnp.concatenate([upper, lower], axis=0)
+        hop(g, 2, right).wait_recv()
+        lower = chip_sum(0, half, tok, cols) + hop_in[2, :, cols].astype(F32)
+        hop(g, 3, left).wait_recv()
+        upper = chip_sum(0, 0, half, cols) + hop_in[3, :, cols].astype(F32)
+        hop(g, 4, right).wait_recv()
+        upper = upper + hop_in[4, :, cols].astype(F32)
+        hop(g, 5, left).wait_recv()
+        lower = lower + hop_in[5, :, cols].astype(F32)
+        done = jnp.concatenate([upper, lower], axis=0)
         if g == 0:
             done = done * cos_ref[...] + pltpu.roll(done, HD // 2, 1) * sin_ref[...]
         packed[:, cols] = dot(place_ref[...], done.astype(BF16)).astype(BF16)
@@ -346,12 +349,10 @@
             for k in routed:
                 route(g, k).wait_send()
             keep(g).wait()
-            for i in range(2, 6):
+            for i in range(6):
                 hop(g, i, right).wait_send()
         for j in range(len(turns)):
             pair(j).wait_send()
-        hop(0, 0, right).wait_send()
-        hop(0, 1, left).wait_send()
 
     @pl.when(sends)
     def _():

time: 57.9 us -> 57 us (0.984)
  Pallas kernels: 55.7 us -> 54.8 us
    pallas_call x1, Pallas kernels: 55.7 us -> 54.8 us  [per_device(): pl.pallas_call(functools.partial(kernel, sizes), out_shape=jax.ShapeDtype...]
where the time goes in v4:
time: 57 us; the launch traced here: 56.8 us
  Pallas kernels  54.8 us (96%)
  between operations  1.3 us (2%)
  local copies, waits for them, and re-layouts  0.68 us (1%)
    pallas_call x1, Pallas kernels, per_device(): pl.pallas_call(functools.partial(kernel, sizes), out_shape=jax.ShapeDtype...  54.8 us

profile of v4, /device:TPU:512, one launch (start us, length us, event | category | flops | bytes accessed | tf_op | source)
XLA Modules:
  0.0 56.8 jit_solution(12637328186505780652)
XLA Ops:
  1.3 54.8 %shard_map.73 = bf16[1,1,384,256]{3,2,1,0:T(8,128)(2,1)S(1)} custom-call(bf16[1,1,256,2048]{3,2,1,0:T(8,128)(2,1)} %hidden.1, s32[1,256]{1,0:T(1,128)} %bitcast.1, s32[1,1]{1,0:T(1,128)S(6)} %copy.9.start, s32[1,1]{1,0:T(1,128)S(6)} %copy.10.live, f32[1,2048]{1,0:T(1,128)} %gain.1, f32[1,128]{1,0:T(1,128)} %constant.2.clone.inverse, ...), custom_call_target="tpu_custom_call" | custom-call | flops 2147483648 | bytes 10485760 | tf_op jit(solution)/shard_map/pallas_call | solution.py:388
  56.1 0.7 %copy.11 = bf16[1,1,384,256]{3,2,1,0:T(8,128)(2,1)} copy(bf16[1,1,384,256]{3,2,1,0:T(8,128)(2,1)S(1)} %shard_map.73) | data formatting | bytes 393216

commit v5 on v4

--- a/solution.py
+++ b/solution.py
@@ -167,6 +167,7 @@
     def _():
         send_meta().start()
         shift(0).start()
+        shift(1).start()
         take(1).wait()
         squares = jnp.zeros((tok, HD), F32)
         for k in range(width // HD):
@@ -175,7 +176,7 @@
         ssq_out[...] = jnp.sum(squares.T, axis=0, keepdims=True)
         for k in range(n_tensor):
             send_ssq(k).start()
-        for i in range(1, len(pieces)):
+        for i in range(2, len(pieces)):
             shift(i).start()
 
     def prepare():
@@ -242,11 +243,12 @@
         shift(len(pieces) - 1).wait_recv()
         activation = normed(at, wide)
         for j, turn in enumerate(turns):
+            if j == 2:
+                far_sums()
             cols = cols_of(turn, 1 - core)
             done = total[:, cols] + dot(activation, w_vmem[at : at + wide, cols])
             pair_out[chip(turn)] = done.astype(BF16)
             pair(j).start()
-        for turn in turns:
             cols = cols_of(turn, core)
             total[:, cols] += dot(activation, w_vmem[at : at + wide, cols])
 
@@ -275,12 +277,14 @@
             hop_out[4 + side, :, parts[g]] = both.astype(BF16)
             hop(g, 4 + side, device).start()
 
-    def ring_sums():
+    def far_sums():
         pair(0).wait_recv()
         hop_out[0] = chip_sum(2, 0, half, everything).astype(BF16)
         hop(0, 0, right).start()
         hop_out[1] = chip_sum(2, half, tok, everything).astype(BF16)
         hop(0, 1, left).start()
+
+    def ring_sums():
         pair(1).wait_recv()
         late_ref[0] = chip_sum(1, 0, half, everything)
         late_ref[2] = chip_sum(1, half, tok, everything)

time: 57 us -> 56.5 us (level)
  no operation moved by 1% of the time
where the time goes in v5:
time: 56.5 us; the launch traced here: 56.3 us
  Pallas kernels  54.4 us (96%)
  between operations  1.3 us (2%)
  local copies, waits for them, and re-layouts  0.68 us (1%)
    pallas_call x1, Pallas kernels, per_device(): pl.pallas_call(functools.partial(kernel, sizes), out_shape=jax.ShapeDtype...  54.4 us

profile of v5, /device:TPU:512, one launch (start us, length us, event | category | flops | bytes accessed | tf_op | source)
XLA Modules:
  0.0 56.3 jit_solution(8597754370087159363)
XLA Ops:
  1.3 54.4 %shard_map.73 = bf16[1,1,384,256]{3,2,1,0:T(8,128)(2,1)S(1)} custom-call(bf16[1,1,256,2048]{3,2,1,0:T(8,128)(2,1)} %hidden.1, s32[1,256]{1,0:T(1,128)} %bitcast.1, s32[1,1]{1,0:T(1,128)S(6)} %copy.9.start, s32[1,1]{1,0:T(1,128)S(6)} %copy.10.live, f32[1,2048]{1,0:T(1,128)} %gain.1, f32[1,128]{1,0:T(1,128)} %constant.2.clone.inverse, ...), custom_call_target="tpu_custom_call" | custom-call | flops 2147483648 | bytes 10485760 | tf_op jit(solution)/shard_map/pallas_call | solution.py:392
  55.7 0.7 %copy.11 = bf16[1,1,384,256]{3,2,1,0:T(8,128)(2,1)} copy(bf16[1,1,384,256]{3,2,1,0:T(8,128)(2,1)S(1)} %shard_map.73) | data formatting | bytes 393216
